TPU v7x, 768 devices: a whole 4x8x12 slice. The times are simulated.
768 devices in a mesh: dp: 32 (over y, x), expert: 24 (over z, core).
Axes of the slice: x: 4, y: 8, z: 12, core: 2. Of those that a mesh axis runs over, the one named last changes fastest.
Arguments:
- tokens: bfloat16 [30720, 2048], P(('dp', 'expert')), may hold values from -6 to 6
- grad_out: bfloat16 [30720, 512], P(('dp', 'expert')), may hold values from -4 to 4
- routes: int32 [30720, 8], P(('dp', 'expert')), may hold values from 0 to 23, all different within a row; in each aligned block of 40 rows (0 to 39, 40 to 79, ...) at most 15 rows name the same one
- combine: bfloat16 [30720, 8], P(('dp', 'expert')), may hold values from 0.049804688 to 0.5
- w_gate: bfloat16 [24, 2048, 512], P('expert'), may hold values from -0.125 to 0.125
- w_up: bfloat16 [24, 2048, 512], P('expert'), may hold values from -0.125 to 0.125
Outputs:
- grad_tokens: bfloat16 [30720, 2048], P(('dp', 'expert'))
- grad_combine: bfloat16 [30720, 8], P(('dp', 'expert'))
- grad_gate: float32 [24, 2048, 512], P('expert', 'dp')
- grad_up: float32 [24, 2048, 512], P('expert', 'dp')
Inputs may be any that keep to these rules, and one draw needn't show every extreme that they name: `routes`: among the rows of one device no expert is chosen more than 15 times; in every draw some expert is chosen exactly 15 times by one device's rows; the 8 experts of a token are different, and every expert is chosen somewhere.
All inputs are finite; a program needn't handle non-finite values.
Results may differ from a plain program's by a relative error of at most 0.02.
Values may be sent and summed in bfloat16 or wider, within the bound.
A program may use at most 64 MiB of HBM per device.

v0:
```python
import jax
import jax.numpy as jnp
from jax import lax
from jax.sharding import PartitionSpec as P


def per_device(tokens, grad_out, routes, combine, w_gate, w_up):
    groups = lax.axis_size("expert")
    local_experts = w_gate.shape[0]
    hidden_units = w_gate.shape[2]
    experts = local_experts * groups
    row_count = tokens.shape[0]
    width = tokens.shape[1]
    picks = routes.shape[1]
    capacity = min(row_count, row_count * picks // experts + 2)
    slot_count = experts * capacity
    chosen = routes.reshape(-1)
    one_hot = (chosen[:, None] == jnp.arange(experts, dtype=jnp.int32)[None, :]).astype(jnp.int32)
    rank_in = jnp.sum((jnp.cumsum(one_hot, axis=0) - one_hot) * one_hot, axis=1)
    slot_ids = chosen * capacity + rank_in
    assign = (jnp.arange(slot_count, dtype=jnp.int32)[:, None] == slot_ids[None, :]).astype(
        jnp.bfloat16
    )
    token_owner = jnp.sum(assign.reshape(slot_count, row_count, picks), axis=2)
    send_rows = jnp.dot(token_owner, tokens, preferred_element_type=jnp.float32).astype(
        jnp.bfloat16
    )
    send_grads = jnp.dot(token_owner, grad_out, preferred_element_type=jnp.float32).astype(
        jnp.bfloat16
    )
    send_weights = jnp.dot(assign, combine.reshape(-1), preferred_element_type=jnp.float32).astype(
        jnp.bfloat16
    )
    block_rows = local_experts * capacity
    recv_rows, recv_grads, recv_weights = (
        lax.all_to_all(
            send_rows.reshape(groups, block_rows, width),
            "expert",
            split_axis=0,
            concat_axis=0,
            tiled=True,
        ),
        lax.all_to_all(
            send_grads.reshape(groups, block_rows, hidden_units),
            "expert",
            split_axis=0,
            concat_axis=0,
            tiled=True,
        ),
        lax.all_to_all(
            send_weights.reshape(groups, block_rows),
            "expert",
            split_axis=0,
            concat_axis=0,
            tiled=True,
        ),
    )
    rows_in = recv_rows.reshape(groups, local_experts, capacity, width)
    grads_in = recv_grads.reshape(groups, local_experts, capacity, hidden_units).astype(jnp.float32)
    weights_in = recv_weights.reshape(groups, local_experts, capacity).astype(jnp.float32)
    gate_pre = jnp.einsum("secd,edf->secf", rows_in, w_gate, preferred_element_type=jnp.float32)
    up_pre = jnp.einsum("secd,edf->secf", rows_in, w_up, preferred_element_type=jnp.float32)
    sigmoid_gate = jax.nn.sigmoid(gate_pre)
    activated = gate_pre * sigmoid_gate
    hidden = activated * up_pre
    upstream = weights_in[..., None] * grads_in
    combine_grad = jnp.sum(hidden * grads_in, axis=3).astype(jnp.bfloat16)
    gate_grad = (upstream * up_pre * sigmoid_gate * (1.0 + gate_pre * (1.0 - sigmoid_gate))).astype(
        jnp.bfloat16
    )
    up_grad = (upstream * activated).astype(jnp.bfloat16)
    input_grad = (
        jnp.einsum("secf,edf->secd", gate_grad, w_gate, preferred_element_type=jnp.float32)
        + jnp.einsum("secf,edf->secd", up_grad, w_up, preferred_element_type=jnp.float32)
    ).astype(jnp.bfloat16)
    back_rows, back_weights = (
        lax.all_to_all(
            input_grad.reshape(groups, block_rows, width),
            "expert",
            split_axis=0,
            concat_axis=0,
            tiled=True,
        ),
        lax.all_to_all(
            combine_grad.reshape(groups, block_rows),
            "expert",
            split_axis=0,
            concat_axis=0,
            tiled=True,
        ),
    )
    grad_tokens = jnp.einsum(
        "st,sd->td",
        token_owner,
        back_rows.reshape(slot_count, width),
        preferred_element_type=jnp.float32,
    ).astype(jnp.bfloat16)
    grad_combine = (
        jnp.einsum(
            "sq,s->q", assign, back_weights.reshape(slot_count), preferred_element_type=jnp.float32
        )
        .astype(jnp.bfloat16)
        .reshape(row_count, picks)
    )
    grad_pair = jnp.stack([gate_grad, up_grad])
    whole_term = jnp.einsum(
        "secd,gsecf->dgef", rows_in, grad_pair, preferred_element_type=jnp.float32
    )
    shares = lax.psum_scatter(
        whole_term.astype(jnp.bfloat16), "dp", scatter_dimension=0, tiled=True
    ).astype(jnp.float32)
    weight_grads = jnp.transpose(shares, (1, 2, 0, 3))
    return (grad_tokens, grad_combine, weight_grads[0], weight_grads[1])


def solution(mesh):
    return jax.shard_map(
        per_device,
        mesh=mesh,
        in_specs=(
            P(("dp", "expert"), None),
            P(("dp", "expert"), None),
            P(("dp", "expert"), None),
            P(("dp", "expert"), None),
            P("expert", None, None),
            P("expert", None, None),
        ),
        out_specs=(
            P(("dp", "expert"), None),
            P(("dp", "expert"), None),
            P("expert", "dp", None),
            P("expert", "dp", None),
        ),
        check_vma=False,
    )
```

profile of v0, /device:TPU:8, one launch (start us, length us, event | category | flops | bytes accessed | tf_op | source)
XLA Modules:
  0.0 354.0 jit_solution(2336782331598912374)
XLA Ops:
  7.2 0.0 copy-start
  7.2 0.9 copy.44
  8.1 0.1 eq.43
  8.2 0.9 reduce-window.6
  9.1 0.2 slice_reduce_fusion
  9.3 0.1 bitcast_bitcast_fusion
  9.5 0.8 copy.48
  10.2 0.1 reshape.133
  10.3 0.2 convolution_reduce_fusion.1
  10.6 0.7 all_to_all.25
  11.3 15.4 %all-to-all-start = ((bf16[24,1,15]{2,1,0:T(2,128)(2,1)}), bf16[24,1,15]{2,1,0:T(2,128)(2,1)S(1)}, u32[]{:S(2)}, u32[]{:S(2)}) async-start(bf16[24,1,15]{2,1,0:T(2,128)(2,1)} %all_to_all.25), calls=%async_computation | async-start | bytes 24576 | tf_op jit(solution)/shard_map/all_to_all | solution.py:50
  26.7 0.1 reduce_sum.33
  26.8 0.2 fusion.32
  27.0 2.6 convolution_convert_fusion
  29.6 2.7 reshape.122
  32.3 0.0 copy-start.3
  32.3 4.2 %all-to-all-done = bf16[24,1,15]{2,1,0:T(2,128)(2,1)S(1)} async-done(((bf16[24,1,15]{2,1,0:T(2,128)(2,1)}), bf16[24,1,15]{2,1,0:T(2,128)(2,1)S(1)}, u32[]{:S(2)}, u32[]{:S(2)}) %all-to-all-start) | async-done | bytes 752 | tf_op jit(solution)/shard_map/all_to_all | solution.py:50
  36.5 5.7 %all-to-all-start.2 = ((bf16[24,15,2048]{2,1,0:T(8,128)(2,1)}), bf16[24,15,2048]{2,1,0:T(8,128)(2,1)}, u32[]{:S(2)}, u32[]{:S(2)}) async-start(bf16[24,15,2048]{2,1,0:T(8,128)(2,1)} %reshape.122), calls=%async_computation.2 | async-start | bytes 3145728 | tf_op jit(solution)/shard_map/all_to_all | solution.py:36
  42.2 0.0 copy-done.3
  42.2 0.3 convolution_convert_fusion.2
  42.5 0.9 reshape.121
  43.4 56.6 %all-to-all-done.2 = bf16[24,15,2048]{2,1,0:T(8,128)(2,1)} async-done(((bf16[24,15,2048]{2,1,0:T(8,128)(2,1)}), bf16[24,15,2048]{2,1,0:T(8,128)(2,1)}, u32[]{:S(2)}, u32[]{:S(2)}) %all-to-all-start.2) | async-done | bytes 1474592 | tf_op jit(solution)/shard_map/all_to_all | solution.py:36
  100.0 4.2 %all-to-all-start.1 = ((bf16[24,15,512]{2,1,0:T(8,128)(2,1)}), bf16[24,15,512]{2,1,0:T(8,128)(2,1)S(1)}, u32[]{:S(2)}, u32[]{:S(2)}) async-start(bf16[24,15,512]{2,1,0:T(8,128)(2,1)} %reshape.121), calls=%async_computation.1 | async-start | bytes 786432 | tf_op jit(solution)/shard_map/all_to_all | solution.py:43
  104.2 3.9 %fusion.12 = f32[24,1,15,512]{3,2,0,1:T(8,128)} fusion(bf16[24,15,2048]{2,1,0:T(8,128)(2,1)} %all-to-all-done.2, bf16[1,2048,512]{2,1,0:T(8,128)(2,1)} %param.10), kind=kOutput, calls=%fused_computation.14 | convolution fusion | flops 754974720 | bytes 4308992 | tf_op jit(solution)/shard_map/secd,edf->secf/dot_general | solution.py:61
  108.2 16.7 %all-to-all-done.1 = bf16[24,15,512]{2,1,0:T(8,128)(2,1)S(1)} async-done(((bf16[24,15,512]{2,1,0:T(8,128)(2,1)}), bf16[24,15,512]{2,1,0:T(8,128)(2,1)S(1)}, u32[]{:S(2)}, u32[]{:S(2)}) %all-to-all-start.1) | async-done | bytes 368672 | tf_op jit(solution)/shard_map/all_to_all | solution.py:43
  124.9 0.0 copy-done
  124.9 0.0 copy-start.1
  124.9 3.1 fusion.23
  128.0 0.0 copy-start.2
  128.1 0.0 copy-done.1
  128.1 2.8 fusion.1
  130.8 0.0 copy-done.2
  130.8 0.1 copy.65
  130.9 0.7 copy.54
  131.6 3.8 %all-to-all-start.4 = ((bf16[24,1,15]{2,1,0:T(2,128)(2,1)}), bf16[24,1,15]{2,1,0:T(2,128)(2,1)S(1)}, u32[]{:S(2)}, u32[]{:S(2)}) async-start(bf16[24,1,15]{2,1,0:T(2,128)(2,1)} %copy.54), calls=%async_computation.4 | async-start | bytes 24576 | tf_op jit(solution)/shard_map/all_to_all | solution.py:84
  135.4 0.0 all-reduce.4.cloned.1.call-start
  135.5 5.9 %fusion = bf16[2048,2,1,512]{0,3,1,2:T(8,128)(2,1)} fusion(bf16[24,15,2048]{2,1,0:T(8,128)(2,1)} %all-to-all-done.2, bf16[1,24,1,15,512]{4,3,1,2,0:T(8,128)(2,1)S(1)} %bitcast.103, bf16[1,24,1,15,512]{4,3,1,2,0:T(8,128)(2,1)} %bitcast.106), kind=kOutput, calls=%fused_computation.1 | convolution fusion | flops 1512415232 | bytes 6406144 | tf_op jit(solution)/shard_map/secd,gsecf->dgef/dot_general | solution.py:106
  141.4 11.1 %copy.57 = bf16[2048,2,1,512]{3,1,2,0:T(2,128)(2,1)} copy(bf16[2048,2,1,512]{0,3,1,2:T(8,128)(2,1)} %fusion) | data formatting | bytes 8388608 | tf_op jit(solution)/shard_map/convert_element_type | solution.py:110
  152.5 0.0 all-reduce.4.cloned.1.call-update
  152.6 2.9 add_convert_fusion
  155.5 2.0 copy.52
  157.5 0.0 all-to-all-done.4
  157.5 9.7 %all-to-all-start.3 = ((bf16[24,15,2048]{2,1,0:T(8,128)(2,1)}), bf16[24,15,2048]{2,1,0:T(8,128)(2,1)}, u32[]{:S(2)}, u32[]{:S(2)}) async-start(bf16[24,15,2048]{2,1,0:T(8,128)(2,1)} %copy.52), calls=%async_computation.3 | async-start | bytes 3145728 | tf_op jit(solution)/shard_map/all_to_all | solution.py:77
  167.2 1.3 dynamic-slice
  169.2 0.1 reshape.137
  169.3 0.2 convolution_reduce_fusion
  169.5 0.1 reshape.129
  169.6 0.7 copy.58
  170.3 169.2 %all-reduce.4.cloned.1.call-done = bf16[2048,2,1,512]{3,1,2,0:T(2,128)(2,1)} async-done(((bf16[2048,2,1,512]{3,1,2,0:T(2,128)(2,1)}), bf16[2048,2,1,512]{3,1,2,0:T(2,128)(2,1)}) %all-reduce.4.cloned.1.call-update) | async-done | bytes 4194320
  339.5 1.0 convert_bitcast_fusion.1
  340.5 0.2 slice_bitcast_fusion
  340.7 0.7 copy.59
  341.4 0.7 copy.60
  342.0 0.0 all-to-all-done.3
  342.0 2.7 reshape.127
  344.7 2.5 convolution_convert_fusion.1
  (8 shorter events, 0.2 us)
Async XLA Ops:
  7.2 117.7 %copy-start = (bf16[1,2048,512]{2,1,0:T(8,128)(2,1)S(1)}, bf16[1,2048,512]{2,1,0:T(8,128)(2,1)}, u32[]{:S(2)}) copy-start(bf16[1,2048,512]{2,1,0:T(8,128)(2,1)} %param.11) | copy-start | bytes 6291460
  11.3 25.2 %all-to-all-start = ((bf16[24,1,15]{2,1,0:T(2,128)(2,1)}), bf16[24,1,15]{2,1,0:T(2,128)(2,1)S(1)}, u32[]{:S(2)}, u32[]{:S(2)}) async-start(bf16[24,1,15]{2,1,0:T(2,128)(2,1)} %all_to_all.25), calls=%async_computation | async-start | bytes 24576 | tf_op jit(solution)/shard_map/all_to_all | solution.py:50
  32.3 9.9 %copy-start.3 = (bf16[40,512]{1,0:T(8,128)(2,1)S(1)}, bf16[40,512]{1,0:T(8,128)(2,1)}, u32[]{:S(2)}) copy-start(bf16[40,512]{1,0:T(8,128)(2,1)} %param.7) | copy-start | bytes 122884
  36.5 63.5 %all-to-all-start.2 = ((bf16[24,15,2048]{2,1,0:T(8,128)(2,1)}), bf16[24,15,2048]{2,1,0:T(8,128)(2,1)}, u32[]{:S(2)}, u32[]{:S(2)}) async-start(bf16[24,15,2048]{2,1,0:T(8,128)(2,1)} %reshape.122), calls=%async_computation.2 | async-start | bytes 3145728 | tf_op jit(solution)/shard_map/all_to_all | solution.py:36
  100.0 24.9 %all-to-all-start.1 = ((bf16[24,15,512]{2,1,0:T(8,128)(2,1)}), bf16[24,15,512]{2,1,0:T(8,128)(2,1)S(1)}, u32[]{:S(2)}, u32[]{:S(2)}) async-start(bf16[24,15,512]{2,1,0:T(8,128)(2,1)} %reshape.121), calls=%async_computation.1 | async-start | bytes 786432 | tf_op jit(solution)/shard_map/all_to_all | solution.py:43
  124.9 3.2 copy-start.1
  128.0 2.8 copy-start.2
  131.6 25.8 %all-to-all-start.4 = ((bf16[24,1,15]{2,1,0:T(2,128)(2,1)}), bf16[24,1,15]{2,1,0:T(2,128)(2,1)S(1)}, u32[]{:S(2)}, u32[]{:S(2)}) async-start(bf16[24,1,15]{2,1,0:T(2,128)(2,1)} %copy.54), calls=%async_computation.4 | async-start | bytes 24576 | tf_op jit(solution)/shard_map/all_to_all | solution.py:84
  135.4 204.0 %all-reduce.4.cloned.1.call-start = ((), (), s32[]{:S(2)}) async-start(), calls=%async_computation.5 | async-start | bytes 8388608
  157.5 184.6 %all-to-all-start.3 = ((bf16[24,15,2048]{2,1,0:T(8,128)(2,1)}), bf16[24,15,2048]{2,1,0:T(8,128)(2,1)}, u32[]{:S(2)}, u32[]{:S(2)}) async-start(bf16[24,15,2048]{2,1,0:T(8,128)(2,1)} %copy.52), calls=%async_computation.3 | async-start | bytes 3145728 | tf_op jit(solution)/shard_map/all_to_all | solution.py:77
Sparse Core Ops, SparseCore 0:
  152.7 186.7 all-reduce.3
where the time goes:
time: 355 us; the launch traced here: 354 us
  waiting for transfers between devices  247 us (70%)
  starting transfers between devices  38.9 us (11%)
  local copies, waits for them, and re-layouts  26.7 us (8%)
  matrix products  24.5 us (7%)
  between operations  14.9 us (4%)
    unnamed x2, waiting for transfers between devices  169 us
    all_to_all x1, waiting for transfers between devices, per_device(): lax.all_to_all(send_rows.reshape(groups, block_rows, width), 'expert', sp...  56.6 us
    all_to_all x1, waiting for transfers between devices, per_device(): lax.all_to_all(send_grads.reshape(groups, block_rows, hidden_units), 'exp...  16.7 us
    all_to_all x1, starting transfers between devices, per_device(): lax.all_to_all(send_weights.reshape(groups, block_rows), 'expert', split_...  15.4 us
    convert_element_type x1, local copies, waits for them, and re-layouts, per_device(): whole_term.astype(jnp.bfloat16)  11.1 us
    all_to_all x1, starting transfers between devices, per_device(): lax.all_to_all(input_grad.reshape(groups, block_rows, width), 'expert', s...  9.74 us
  transfers between devices with their start and end apart: 6, of which 4 were waited for; matrix products, arithmetic and copies ran while one was open for 11% of the time, Pallas kernels for 0%

commit v1 on v0

v1 whole, which is shorter than its diff:
```python
import functools

import jax
import jax.numpy as jnp
from jax import lax
from jax.experimental import pallas as pl
from jax.experimental.pallas import tpu as pltpu
from jax.sharding import PartitionSpec as P

F32 = jnp.float32
BF16 = jnp.bfloat16
MESH = pl.DeviceIdType.MESH

NX, NY, NZ = 4, 8, 12
TOK = 40
DM = 2048
FF = 512
AG_ROWS = (416, 400)
RS_ROWS = (336, 320)
CA = 640
CB = 2 * FF - CA
NT = (((1,), (1,)), ((), ()))
TN = (((0,), (0,)), ((), ()))


def dot(a, b, dims=(((1,), (0,)), ((), ()))):
    return lax.dot_general(a, b, dims, preferred_element_type=F32)


def iota(shape, dim):
    return lax.broadcasted_iota(jnp.int32, shape, dim)


def kernel(
    tok, go, routes, comb, wg, wu,
    gt, gc, dg, du,
    ZR, ZS, X, GU, WC, OWN, SND, SIB, RP, RM,
    PA, PB, AX1, AX2, SA, SAB, AY1, AY, BY, SB, SBB, BX1, BX2, BXS,
    w_sem,
    ag_send, zr_recv, sf_send, zs_recv, snd_send, sib_recv, rs_send, rs_recv,
    ax1_send, ax1_recv, ax2_send, ax2_recv, ay_send, ay_recv, by_send, by_recv,
    bx1_send, bx1_recv, bx2_send, bx2_recv,
):
    dp = lax.axis_index("dp")
    ex = lax.axis_index("expert")
    x, y = lax.rem(dp, NX), dp // NX
    core, z = lax.rem(ex, 2), ex // 2

    def xdev(step):
        return (y * NX + lax.rem(x + step + NX, NX), ex)

    def ydev(step):
        return (lax.rem(y + step + NY, NY) * NX + x, ex)

    def zdev(step):
        return (dp, lax.rem(z + step + NZ, NZ) * 2 + core)

    sib = (dp, z * 2 + 1 - core)

    def remote(src, dst, ssem, rsem, dev):
        return pltpu.make_async_remote_copy(
            src_ref=src, dst_ref=dst, send_sem=ssem, recv_sem=rsem,
            device_id=dev, device_id_type=MESH,
        )

    load_g = pltpu.make_async_copy(wg.at[0], WC.at[:, pl.ds(0, FF)], w_sem.at[0])
    load_u = pltpu.make_async_copy(wu.at[0], WC.at[:, pl.ds(FF, FF)], w_sem.at[1])
    load_g.start()
    load_u.start()

    barrier = pltpu.get_barrier_semaphore()
    for dev in (zdev(1), zdev(-1), sib, xdev(1), xdev(-1), ydev(1), ydev(-1)):
        pl.semaphore_signal(barrier, inc=1, device_id=dev, device_id_type=MESH)

    tf = tok[...].astype(F32)
    gf = go[...].astype(F32)
    for j in range(2):
        for b in range(4):
            lo = j * 512 + b * 128
            ZR[0, j, pl.ds(80 * b, 80), :] = jnp.concatenate(
                [tf[:, lo:lo + 128], tf[:, 1024 + lo:1024 + lo + 128]], axis=0
            ).astype(BF16)
        ZR[0, j, pl.ds(320, 80), :] = jnp.concatenate(
            [gf[:, j * 128:j * 128 + 128], gf[:, 256 + j * 128:256 + j * 128 + 128]], axis=0
        ).astype(BF16)

    rt = routes[...]
    cf = comb[...].astype(F32)
    lane = iota((TOK, 128), 1)
    dense = jnp.zeros((TOK, 128), F32)
    for k in range(8):
        dense = dense + jnp.where(rt[:, k:k + 1] == lane, cf[:, k:k + 1], 0.0)
    dense = jnp.concatenate([dense, jnp.zeros((128 - TOK, 128), F32)], axis=0).astype(BF16)
    r16, l16 = iota((16, 128), 0), iota((16, 128), 1)
    r128, l128 = iota((128, 128), 0), iota((128, 128), 1)
    even = dot((l16 == 2 * r16).astype(BF16), dense, NT)
    odd = dot((l16 == 2 * r16 + 1).astype(BF16), dense, NT).astype(BF16)
    odd = dot(odd, (l128 == r128 + TOK).astype(BF16))
    ZR[0, 0, pl.ds(400, 16), :] = (even + odd).astype(BF16)

    pick = lane == core * TOK + iota((TOK, 128), 0)

    def ag(p, k, j):
        rows = pl.ds(0, AG_ROWS[j])
        if p:
            src, dst = lax.rem(13 - k, NZ), NZ - k
        else:
            src, dst = k - 1, k
        return remote(
            ZR.at[src, j, rows], ZR.at[dst, j, rows],
            ag_send.at[p, k - 1, j], zr_recv.at[dst, j], zdev(1 if p else -1),
        )

    def share(r, j):
        rows = pl.ds(0, AG_ROWS[j])
        return remote(ZR.at[r, j, rows], ZS.at[r, j, rows], sf_send.at[r, j], zs_recv.at[r, j], sib)

    def give(r, j):
        rows = pl.ds(0, RS_ROWS[j])
        return remote(SND.at[r, j, rows], SIB.at[r, j, rows], snd_send.at[r, j], sib_recv.at[r, j], sib)

    def rs(p, k, j):
        rows = pl.ds(0, RS_ROWS[j])
        src = k if p else NZ - k
        land = RP if p else RM
        return remote(
            OWN.at[src, j, rows], land.at[k - 1, j, rows],
            rs_send.at[p, k - 1, j], rs_recv.at[p, k - 1, j], zdev(1 if p else -1),
        )

    pl.semaphore_wait(barrier, 7)

    for p, j in ((1, 0), (0, 1), (1, 1), (0, 0)):
        ag(p, 1, j).start()
    share(0, 0).start()
    share(0, 1).start()
    load_g.wait()
    load_u.wait()

    def rows_of(ref, slots, j, lo):
        top, low = [], []
        for r in slots:
            for buf in (ZR, ZS):
                block = buf[r, j, pl.ds(lo, 80), :].astype(F32)
                top.append(block[:TOK])
                low.append(block[TOK:])
        return jnp.concatenate(top, axis=0), jnp.concatenate(low, axis=0)

    def first(slots, row0):
        n = 80 * len(slots)
        rows = pl.ds(row0, n)
        for r in slots:
            for j in range(2):
                share(r, j).wait_recv()
        for j in range(2):
            for b in range(4):
                top, low = rows_of(None, slots, j, 80 * b)
                X[rows, pl.ds(j * 512 + b * 128, 128)] = top.astype(BF16)
                X[rows, pl.ds(1024 + j * 512 + b * 128, 128)] = low.astype(BF16)
        g0 = rows_of(None, slots, 0, 320)
        g1 = rows_of(None, slots, 1, 320)
        weights = []
        for r in slots:
            for buf in (ZR, ZS):
                tile = buf[r, 0, pl.ds(400, 16), :].astype(F32)
                line = jnp.sum(jnp.where(r16 == z, tile, 0.0), axis=0, keepdims=True)
                weights.append(jnp.sum(jnp.where(pick, line, 0.0), axis=1, keepdims=True))
        weight = jnp.concatenate(weights, axis=0)
        total = jnp.zeros((n, 1), F32)
        for t in range(2):
            cot = jnp.concatenate([g0[t], g1[t]], axis=1)
            xs = X[rows, :]
            gate = dot(xs, WC[:, pl.ds(256 * t, 256)])
            up = dot(xs, WC[:, pl.ds(FF + 256 * t, 256)])
            sig = 1.0 / (1.0 + jnp.exp(-gate))
            act = gate * sig
            total = total + jnp.sum(act * up * cot, axis=1, keepdims=True)
            ups = weight * cot
            GU[rows, pl.ds(256 * t, 256)] = (
                ups * up * sig * (1.0 + gate * (1.0 - sig))
            ).astype(BF16)
            GU[rows, pl.ds(FF + 256 * t, 256)] = (ups * act).astype(BF16)
        i = 0
        for r in slots:
            for buf in (OWN, SND):
                line = jnp.sum(
                    jnp.where(pick, total[TOK * i:TOK * i + TOK], 0.0), axis=0, keepdims=True
                )
                buf[r, 0, pl.ds(320, 16), :] = jnp.where(r16 == z, line, 0.0).astype(BF16)
                i += 1

    def second(slots, row0):
        n = 80 * len(slots)
        grads = GU[pl.ds(row0, n), :]
        for j in range(2):
            top = dot(grads, WC[pl.ds(j * 512, 512), :], NT)
            low = dot(grads, WC[pl.ds(1024 + j * 512, 512), :], NT)
            i = 0
            for r in slots:
                for buf in (OWN, SND):
                    for b in range(4):
                        buf[r, j, pl.ds(80 * b, 80), :] = jnp.concatenate(
                            [
                                top[TOK * i:TOK * i + TOK, 128 * b:128 * b + 128],
                                low[TOK * i:TOK * i + TOK, 128 * b:128 * b + 128],
                            ],
                            axis=0,
                        ).astype(BF16)
                    i += 1
                give(r, j).start()

    def arrive(k, stage):
        for p in (1, 0):
            j = stage if p else 1 - stage
            ag(p, k, j).wait_recv()
            if stage == 0:
                ag(p, k + 1, j).start()
            else:
                @pl.when(k < 5)
                def _():
                    ag(p, k + 1, j).start()
            share(NZ - k if p else k, j).start()

    one, zero = jnp.int32(1), jnp.int32(0)
    arrive(1, 0)
    first([0], 0)
    arrive(1, 1)
    second([0], 0)

    def gather_step(k, carry):
        row0 = pl.multiple_of(80 + 160 * (k - 2), 16)
        arrive(k, 0)
        first([NZ + 1 - k, k - 1], row0)
        arrive(k, 1)
        second([NZ + 1 - k, k - 1], row0)
        return carry

    lax.fori_loop(2, 6, gather_step, 0)
    first([7, 5], 720)
    for p in (1, 0):
        j = 0 if p else 1
        ag(p, 6, j).wait_recv()
        share(6, j).start()
    first([6], 880)

    def weight_rows(dy):
        col = pl.multiple_of(lax.rem(y + dy, NY) * 256, 256)
        xs = X[:, pl.ds(col, 256)]
        PA[dy] = dot(xs, GU[:, pl.ds(0, CA)], TN).astype(BF16)
        PB[dy] = dot(xs, GU[:, pl.ds(CA, CB)], TN).astype(BF16)

    def xrow(step):
        return lax.rem(x + step, NX) * 64

    def near(p):
        return 1 if p else NX - 1

    def ax1(p, dy):
        row = pl.multiple_of(xrow(2) + (0 if p else 32), 32)
        return remote(
            PA.at[dy, pl.ds(row, 32)], AX1.at[p, dy], ax1_send.at[p, dy], ax1_recv.at[p, dy],
            xdev(1 if p else -1),
        )

    def ax2(p, dy):
        row = pl.multiple_of(xrow(near(p)), 64)
        return remote(
            PA.at[dy, pl.ds(row, 64)], AX2.at[p, dy], ax2_send.at[p, dy], ax2_recv.at[p, dy],
            xdev(1 if p else -1),
        )

    def a_open(dy):
        weight_rows(dy)
        ax1(1, dy).start()
        ax1(0, dy).start()

    def a_pass(dy):
        for p in (1, 0):
            ax1(p, dy).wait_recv()
            row = pl.multiple_of(xrow(near(p)) + (0 if p else 32), 32)
            PA[dy, pl.ds(row, 32), :] = (
                PA[dy, pl.ds(row, 32), :].astype(F32) + AX1[p, dy].astype(F32)
            ).astype(BF16)
            ax2(p, dy).start()

    def a_sum(dy):
        ax2(1, dy).wait_recv()
        ax2(0, dy).wait_recv()
        row = pl.multiple_of(x * 64, 64)
        SA[dy] = (
            PA[dy, pl.ds(row, 64), :].astype(F32)
            + AX2[1, dy].astype(F32) + AX2[0, dy].astype(F32)
        )

    def ay1(p):
        return remote(
            SAB.at[4, pl.ds(0 if p else 32, 32)], AY1.at[p], ay_send.at[p, 3], ay_recv.at[p, 3],
            ydev(1 if p else -1),
        )

    def ay(p, k):
        return remote(
            SAB.at[k if p else NY - k], AY.at[p, k - 1], ay_send.at[p, k - 1],
            ay_recv.at[p, k - 1], ydev(1 if p else -1),
        )

    def ay_first():
        SAB[4] = SA[4].astype(BF16)
        ay1(1).start()
        ay1(0).start()

    def ay_pass(k):
        for p in (1, 0):
            dy = k if p else NY - k
            if k == 3:
                ay1(p).wait_recv()
                lo = 0 if p else 32
                SAB[dy, pl.ds(32 - lo, 32), :] = SA[dy, pl.ds(32 - lo, 32), :].astype(BF16)
                SAB[dy, pl.ds(lo, 32), :] = (
                    SA[dy, pl.ds(lo, 32), :] + AY1[p].astype(F32)
                ).astype(BF16)
            else:
                ay(p, k + 1).wait_recv()
                SAB[dy] = (SA[dy] + AY[p, k].astype(F32)).astype(BF16)
            ay(p, k).start()

    def by(p, k, s):
        dy = k if p else NY - k
        return remote(
            PB.at[dy, pl.ds(128 * s, 128)], BY.at[p, k - 1, s], by_send.at[p, k - 1, s],
            by_recv.at[p, k - 1, s], ydev(1 if p else -1),
        )

    def b_pass(p, k, s):
        by(p, k + 1, s).wait_recv()
        dy = k if p else NY - k
        rows = pl.ds(128 * s, 128)
        PB[dy, rows, :] = (PB[dy, rows, :].astype(F32) + BY[p, k, s].astype(F32)).astype(BF16)
        by(p, k, s).start()

    def b_sum():
        for s in (1, 0):
            by(1, 1, s).wait_recv()
            by(0, 1, s).wait_recv()
            rows = pl.ds(128 * s, 128)
            SB[rows, :] = (
                PB[0, rows, :].astype(F32) + BY[1, 0, s].astype(F32) + BY[0, 0, s].astype(F32)
            )
        row = pl.multiple_of(xrow(2), 64)
        SBB[...] = SB[pl.ds(row, 64), :].astype(BF16)

    def bx1(p):
        return remote(
            SBB.at[pl.ds(0 if p else 32, 32)], BX1.at[p], bx1_send.at[p], bx1_recv.at[p],
            xdev(1 if p else -1),
        )

    def bx2(p):
        return remote(
            BXS.at[p], BX2.at[p], bx2_send.at[p], bx2_recv.at[p], xdev(1 if p else -1)
        )

    def bx_pass():
        for p in (1, 0):
            row = pl.multiple_of(xrow(near(p)), 64)
            mine = SB[pl.ds(row, 64), :]
            bx1(p).wait_recv()
            lo = 0 if p else 32
            BXS[p, pl.ds(32 - lo, 32), :] = mine[32 - lo:64 - lo].astype(BF16)
            BXS[p, pl.ds(lo, 32), :] = (mine[lo:lo + 32] + BX1[p].astype(F32)).astype(BF16)
            bx2(p).start()

    def mix(r, j):
        rows = pl.ds(0, RS_ROWS[j])
        return OWN[r, j, rows, :].astype(F32) + SIB[r, j, rows, :].astype(F32)

    def z_pass(p, k, j):
        r = k if p else NZ - k
        rows = pl.ds(0, RS_ROWS[j])
        give(r, j).wait_recv()
        total = mix(r, j)
        if k < 5 or (k == 5 and j == 1 - p):
            rs(p, k + 1, j).wait_recv()
            land = RP if p else RM
            total = total + land[k, j, rows, :].astype(F32)
        OWN[r, j, rows, :] = total.astype(BF16)
        rs(p, k, j).start()

    def z_step(k):
        for p, j in ((1, 1), (0, 0), (1, 0), (0, 1)):
            z_pass(p, k, j)

    a_open(4)
    by(1, 4, 0).start()
    by(0, 4, 1).start()
    second([7, 5, 6], 720)
    a_open(3)
    by(1, 3, 1).start()
    a_open(5)
    by(0, 3, 0).start()
    z_pass(1, 6, 0)
    z_pass(0, 6, 1)
    z_pass(1, 5, 1)
    z_pass(0, 5, 0)
    a_pass(4)
    b_pass(1, 3, 0)
    b_pass(0, 3, 1)
    a_open(2)
    a_open(6)
    z_pass(1, 5, 0)
    z_pass(0, 5, 1)
    a_pass(3)
    a_pass(5)
    a_sum(4)
    ay_first()
    for p, s in ((1, 1), (0, 0), (1, 0), (0, 1)):
        b_pass(p, 2, s)
    a_open(1)
    a_open(7)
    z_step(4)
    a_pass(2)
    a_pass(6)
    a_sum(3)
    a_sum(5)
    ay_pass(3)
    a_open(0)
    for p, s in ((1, 1), (0, 0), (1, 0), (0, 1)):
        b_pass(p, 1, s)
    z_step(3)
    a_pass(1)
    a_pass(7)
    a_sum(2)
    a_sum(6)
    ay_pass(2)
    b_sum()
    bx1(1).start()
    bx1(0).start()
    z_step(2)
    a_pass(0)
    a_sum(1)
    a_sum(7)
    ay_pass(1)
    bx_pass()
    z_step(1)

    a_sum(0)
    bx2(1).wait_recv()
    bx2(0).wait_recv()
    row = pl.multiple_of(x * 64, 64)
    du[:, pl.ds(CA - FF, CB)] = (
        SB[pl.ds(row, 64), :] + BX2[1].astype(F32) + BX2[0].astype(F32)
    )

    for j in (1, 0):
        rows = pl.ds(0, RS_ROWS[j])
        give(0, j).wait_recv()
        rs(1, 1, j).wait_recv()
        rs(0, 1, j).wait_recv()
        total = mix(0, j) + RP[0, j, rows, :].astype(F32) + RM[0, j, rows, :].astype(F32)
        for b in range(4):
            lo = j * 512 + b * 128
            gt[:, pl.ds(lo, 128)] = total[80 * b:80 * b + TOK].astype(BF16)
            gt[:, pl.ds(1024 + lo, 128)] = total[80 * b + TOK:80 * b + 80].astype(BF16)
        if j == 0:
            back = jnp.concatenate([total[320:336], jnp.zeros((112, 128), F32)], axis=0).astype(BF16)
            spread = jnp.zeros((TOK, 128), F32)
            for c in range(2):
                line = dot(
                    (lane == iota((TOK, 128), 0) + c * TOK).astype(BF16), back, NT
                ).astype(BF16)
                spread = spread + dot(line, (l128 == 2 * r128 + c).astype(BF16))
            out = jnp.zeros((TOK, 8), F32)
            lane8 = iota((TOK, 8), 1)
            for k in range(8):
                value = jnp.sum(
                    jnp.where(rt[:, k:k + 1] == lane, spread, 0.0), axis=1, keepdims=True
                )
                out = out + jnp.where(lane8 == k, value, 0.0)
            gc[...] = out.astype(BF16)

    ay(1, 1).wait_recv()
    ay(0, 1).wait_recv()
    total = SA[0] + AY[1, 0].astype(F32) + AY[0, 0].astype(F32)
    dg[...] = total[:, :FF]
    du[:, pl.ds(0, CA - FF)] = total[:, FF:]

    for p in (1, 0):
        for k in range(1, 7):
            for j in range(2):
                if k < 6 or j == 1 - p:
                    ag(p, k, j).wait_send()
                    rs(p, k, j).wait_send()
        for dy in range(NY):
            ax1(p, dy).wait_send()
            ax2(p, dy).wait_send()
        ay1(p).wait_send()
        for k in range(1, 4):
            ay(p, k).wait_send()
            for s in range(2):
                by(p, k, s).wait_send()
        by(p, 4, 1 - p).wait_send()
        bx1(p).wait_send()
        bx2(p).wait_send()
    for r in range(NZ):
        for j in range(2):
            share(r, j).wait_send()
            give(r, j).wait_send()


def per_device(tokens, grad_out, routes, combine, w_gate, w_up):
    vm = pl.BlockSpec(memory_space=pltpu.VMEM)
    hbm = pl.BlockSpec(memory_space=pl.ANY)
    V = pltpu.VMEM
    S = pltpu.SemaphoreType.DMA
    out = pl.pallas_call(
        kernel,
        out_shape=(
            jax.ShapeDtypeStruct((TOK, DM), BF16),
            jax.ShapeDtypeStruct((TOK, 8), BF16),
            jax.ShapeDtypeStruct((64, FF), F32),
            jax.ShapeDtypeStruct((64, FF), F32),
        ),
        in_specs=[vm, vm, vm, vm, hbm, hbm],
        out_specs=(vm, vm, vm, vm),
        scratch_shapes=[
            V((NZ, 2, 416, 128), BF16),
            V((NZ, 2, 416, 128), BF16),
            V((NZ * 80, DM), BF16),
            V((NZ * 80, 2 * FF), BF16),
            V((DM, 2 * FF), BF16),
            V((NZ, 2, 336, 128), BF16),
            V((NZ, 2, 336, 128), BF16),
            V((NZ, 2, 336, 128), BF16),
            V((6, 2, 336, 128), BF16),
            V((6, 2, 336, 128), BF16),
            V((NY, 256, CA), BF16),
            V((NY, 256, CB), BF16),
            V((2, NY, 32, CA), BF16),
            V((2, NY, 64, CA), BF16),
            V((NY, 64, CA), F32),
            V((NY, 64, CA), BF16),
            V((2, 32, CA), BF16),
            V((2, 3, 64, CA), BF16),
            V((2, 4, 2, 128, CB), BF16),
            V((256, CB), F32),
            V((64, CB), BF16),
            V((2, 32, CB), BF16),
            V((2, 64, CB), BF16),
            V((2, 64, CB), BF16),
            S((2,)),
            S((2, 6, 2)), S((NZ, 2)), S((NZ, 2)), S((NZ, 2)), S((NZ, 2)), S((NZ, 2)),
            S((2, 6, 2)), S((2, 6, 2)),
            S((2, NY)), S((2, NY)), S((2, NY)), S((2, NY)), S((2, 4)), S((2, 4)),
            S((2, 4, 2)), S((2, 4, 2)),
            S((2,)), S((2,)), S((2,)), S((2,)),
        ],
        compiler_params=pltpu.CompilerParams(
            collective_id=0, has_side_effects=True, vmem_limit_bytes=56 * 2**20
        ),
    )(tokens, grad_out, routes, combine, w_gate, w_up)
    return out[0], out[1], out[2][None], out[3][None]


def solution(mesh):
    return jax.shard_map(
        per_device,
        mesh=mesh,
        in_specs=(
            P(("dp", "expert"), None),
            P(("dp", "expert"), None),
            P(("dp", "expert"), None),
            P(("dp", "expert"), None),
            P("expert", None, None),
            P("expert", None, None),
        ),
        out_specs=(
            P(("dp", "expert"), None),
            P(("dp", "expert"), None),
            P("expert", "dp", None),
            P("expert", "dp", None),
        ),
        check_vma=False,
    )
```

time: 355 us -> 95.7 us (0.27)
  the two profiles are of different devices: /device:TPU:8 before, /device:TPU:16 now
where the time goes in v1:
time: 95.7 us; the launch traced here: 95.3 us
  Pallas kernels  85.9 us (90%)
  local copies, waits for them, and re-layouts  8.8 us (9%)
    pallas_call x1, Pallas kernels, per_device(): pl.pallas_call(kernel, out_shape=(jax.ShapeDtypeStruct((TOK, DM), BF16),...  85.9 us
    unnamed x6, local copies, waits for them, and re-layouts  8.8 us

profile of v1, /device:TPU:16, one launch (start us, length us, event | category | flops | bytes accessed | tf_op | source)
XLA Modules:
  0.0 95.3 jit_solution(13159017313016807641)
XLA Ops:
  0.6 1.4 %copy.11.comb = bf16[40,8]{1,0:T(8,128)(2,1)} copy(bf16[40,8]{0,1:T(8,128)(2,1)} %param.9) | data formatting | bytes 1280 | tf_op args[3]
  2.0 1.4 %copy.10.routes = s32[40,8]{1,0:T(8,128)} copy(s32[40,8]{0,1:T(8,128)} %param.8) | data formatting | bytes 2560 | tf_op args[2]
  3.4 85.9 %shard_map.93 = (bf16[40,2048]{1,0:T(8,128)(2,1)}, bf16[40,8]{1,0:T(8,128)(2,1)}, f32[64,512]{1,0:T(8,128)}, f32[64,512]{1,0:T(8,128)}) custom-call(bf16[40,2048]{1,0:T(8,128)(2,1)} %tok.1, bf16[40,512]{1,0:T(8,128)(2,1)} %go.1, s32[40,8]{1,0:T(8,128)} %copy.10.routes, bf16[40,8]{1,0:T(8,128)(2,1)} %copy.11.comb, bf16[1,2048,512]{2,1,0:T(8,128)(2,1)} %wg.1, ...), custom_call_target="tpu_custom_call" | custom-call | tf_op jit(solution)/shard_map/pallas_call | solution.py:515
  89.3 1.4 %copy.12 = bf16[40,8]{0,1:T(8,128)(2,1)} copy(bf16[40,8]{1,0:T(8,128)(2,1)} %get-tuple-element.13) | data formatting | bytes 1280
  90.6 1.6 %copy.16 = bf16[40,2048]{1,0:T(8,128)(2,1)} copy(bf16[40,2048]{1,0:T(8,128)(2,1)} %get-tuple-element.20) | data formatting | bytes 327680
  92.2 1.6 %copy.17 = f32[1,64,512]{2,1,0:T(8,128)} copy(f32[1,64,512]{2,1,0:T(8,128)} %bitcast.3) | data formatting | bytes 262144
  93.8 1.6 %copy.18 = f32[1,64,512]{2,1,0:T(8,128)} copy(f32[1,64,512]{2,1,0:T(8,128)} %bitcast.2) | data formatting | bytes 262144

commit v2 on v1

v2 whole, which is shorter than its diff:
```python
import functools

import jax
import jax.numpy as jnp
from jax import lax
from jax.experimental import pallas as pl
from jax.experimental.pallas import tpu as pltpu
from jax.sharding import PartitionSpec as P

F32 = jnp.float32
BF16 = jnp.bfloat16
MESH = pl.DeviceIdType.MESH

NX, NY, NZ = 4, 8, 12
TOK = 40
DM = 2048
FF = 512
AG_ROWS = (416, 400)
RS_ROWS = (336, 320)
CA = 640
CB = 2 * FF - CA
ORDER = (
    ("F6",), ("W", 4), ("BY", 1, 4, 0), ("BY", 0, 4, 1), ("S6",), ("W", 3), ("W", 5),
    ("A2", 1, 4), ("A2", 0, 4), ("BY", 1, 3, 1), ("BY", 0, 3, 0), ("Z", 1, 6, 1), ("Z", 1, 6, 0),
    ("Z", 0, 6, 2), ("Z", 0, 6, 3), ("BY", 1, 3, 0), ("BY", 0, 3, 1), ("W", 2), ("W", 6),
    ("A2", 1, 3), ("A2", 0, 3), ("A2", 1, 5), ("A2", 0, 5), ("Z", 1, 5, 1), ("Z", 0, 5, 1),
    ("Z", 1, 5, 0), ("Z", 1, 5, 2), ("Z", 1, 5, 3), ("Z", 0, 5, 0), ("Z", 0, 5, 2),
    ("Z", 0, 5, 3), ("A3", 4), ("BY", 1, 2, 1), ("BY", 0, 2, 0), ("W", 1), ("BY", 1, 2, 0),
    ("BY", 0, 2, 1), ("Z", 1, 4, 1), ("Z", 0, 4, 1), ("W", 7), ("Z", 1, 4, 0), ("Z", 0, 4, 0),
    ("A3", 3), ("Z", 1, 4, 2), ("Z", 0, 4, 2), ("A2", 1, 2), ("A2", 0, 2), ("A2", 1, 6),
    ("A2", 0, 6), ("Z", 1, 4, 3), ("Z", 0, 4, 3), ("A3", 5), ("AY", 1, 3), ("AY", 0, 3),
    ("BY", 1, 1, 1), ("BY", 0, 1, 0), ("Z", 1, 3, 1), ("Z", 0, 3, 1), ("W", 0), ("Z", 1, 3, 0),
    ("Z", 0, 3, 0), ("BY", 1, 1, 0), ("BY", 0, 1, 1), ("Z", 1, 3, 2), ("Z", 0, 3, 2),
    ("A2", 1, 1), ("A2", 0, 1), ("A3", 2), ("Z", 1, 3, 3), ("Z", 0, 3, 3), ("A2", 1, 7),
    ("A2", 0, 7), ("AY", 1, 2), ("Z", 1, 2, 1), ("Z", 0, 2, 1), ("A3", 6), ("AY", 0, 2),
    ("Z", 1, 2, 0), ("Z", 0, 2, 0), ("A2", 1, 0), ("A2", 0, 0), ("Z", 1, 2, 2), ("Z", 0, 2, 2),
    ("Z", 1, 2, 3), ("Z", 0, 2, 3), ("A3", 1), ("Z", 1, 1, 1), ("Z", 0, 1, 1), ("BS",),
    ("Z", 1, 1, 0), ("Z", 0, 1, 0), ("A3", 7), ("Z", 1, 1, 2), ("Z", 0, 1, 2), ("AY", 1, 1),
    ("AY", 0, 1), ("Z", 1, 1, 3), ("Z", 0, 1, 3), ("A3", 0), ("BX", 1), ("BX", 0), ("ZF", 1),
    ("ZF", 0), ("ZF", 2), ("AF",), ("ZF", 3), ("BF",),
)
NT = (((1,), (1,)), ((), ()))
TN = (((0,), (0,)), ((), ()))


def dot(a, b, dims=(((1,), (0,)), ((), ()))):
    return lax.dot_general(a, b, dims, preferred_element_type=F32)


def iota(shape, dim):
    return lax.broadcasted_iota(jnp.int32, shape, dim)


def kernel(
    tok_in, go_in, routes_in, comb_in, wg, wu,
    gt_out, gc_out, dg_out, du_out,
    tok, go, routes, comb, gt, gc, dg, du,
    ZR, ZS, X, GU, WC, OWN, SND, SIB, RP, RM,
    PA, PB, AX1, AX2, SA, SAB, AY1, AY, BY, SB, SBB, BX1, BX2, BXS,
    w_sem, in_sem, out_sem,
    ag_send, zr_recv, sf_send, zs_recv, snd_send, sib_recv, rs_send, rs_recv,
    ax1_send, ax1_recv, ax2_send, ax2_recv, ay_send, ay_recv, by_send, by_recv,
    bx1_send, bx1_recv, bx2_send, bx2_recv,
):
    dp = lax.axis_index("dp")
    ex = lax.axis_index("expert")
    x, y = lax.rem(dp, NX), dp // NX
    core, z = lax.rem(ex, 2), ex // 2

    def xdev(step):
        return (y * NX + lax.rem(x + step + NX, NX), ex)

    def ydev(step):
        return (lax.rem(y + step + NY, NY) * NX + x, ex)

    def zdev(step):
        return (dp, lax.rem(z + step + NZ, NZ) * 2 + core)

    sib = (dp, z * 2 + 1 - core)

    def remote(src, dst, ssem, rsem, dev):
        return pltpu.make_async_remote_copy(
            src_ref=src, dst_ref=dst, send_sem=ssem, recv_sem=rsem,
            device_id=dev, device_id_type=MESH,
        )

    barrier = pltpu.get_barrier_semaphore()
    for dev in (zdev(1), zdev(-1), sib, xdev(1), xdev(-1), ydev(1), ydev(-1)):
        pl.semaphore_signal(barrier, inc=1, device_id=dev, device_id_type=MESH)

    loads = [
        pltpu.make_async_copy(src, dst, in_sem.at[i])
        for i, (src, dst) in enumerate(
            ((tok_in, tok), (go_in, go), (routes_in, routes), (comb_in, comb))
        )
    ]
    stores = [
        pltpu.make_async_copy(src, dst, out_sem.at[i])
        for i, (src, dst) in enumerate(((gt, gt_out), (gc, gc_out), (dg, dg_out), (du, du_out)))
    ]
    load_g = pltpu.make_async_copy(wg.at[0], WC.at[:, pl.ds(0, FF)], w_sem.at[0])
    load_u = pltpu.make_async_copy(wu.at[0], WC.at[:, pl.ds(FF, FF)], w_sem.at[1])
    for load in loads:
        load.start()
    load_g.start()
    load_u.start()
    for load in loads:
        load.wait()

    tf = tok[...].astype(F32)
    gf = go[...].astype(F32)
    for j in range(2):
        for b in range(4):
            lo = j * 512 + b * 128
            ZR[0, j, pl.ds(80 * b, 80), :] = jnp.concatenate(
                [tf[:, lo:lo + 128], tf[:, 1024 + lo:1024 + lo + 128]], axis=0
            ).astype(BF16)
        ZR[0, j, pl.ds(320, 80), :] = jnp.concatenate(
            [gf[:, j * 128:j * 128 + 128], gf[:, 256 + j * 128:256 + j * 128 + 128]], axis=0
        ).astype(BF16)

    rt = routes[...]
    cf = comb[...].astype(F32)
    r16, r40 = iota((16, TOK), 0), iota((TOK, 128), 0)
    lane = iota((TOK, 128), 1)
    r16w = iota((16, 128), 0)
    spots = [(lane == r40 + c * TOK).astype(BF16) for c in range(2)]
    tile = jnp.zeros((16, 128), F32)
    for c in range(2):
        dense = jnp.zeros((16, TOK), F32)
        for k in range(8):
            dense = dense + jnp.where(rt[k:k + 1, :] == 2 * r16 + c, cf[k:k + 1, :], 0.0)
        tile = tile + dot(dense.astype(BF16), spots[c])
    ZR[0, 0, pl.ds(400, 16), :] = tile.astype(BF16)

    pick = lane == core * TOK + r40

    def ag(p, k, q):
        j, h = q // 2, q % 2
        rows = pl.ds(208 * h, AG_ROWS[j] - 208 if h else 208)
        if p:
            src, dst = lax.rem(13 - k, NZ), NZ - k
        else:
            src, dst = k - 1, k
        return remote(
            ZR.at[src, j, rows], ZR.at[dst, j, rows],
            ag_send.at[p, k - 1, q], zr_recv.at[dst, q], zdev(1 if p else -1),
        )

    def share(r, j):
        rows = pl.ds(0, AG_ROWS[j])
        return remote(ZR.at[r, j, rows], ZS.at[r, j, rows], sf_send.at[r, j], zs_recv.at[r, j], sib)

    def give(r, j):
        rows = pl.ds(0, RS_ROWS[j])
        return remote(SND.at[r, j, rows], SIB.at[r, j, rows], snd_send.at[r, j], sib_recv.at[r, j], sib)

    def part(q):
        return q // 2, pl.ds(160 * (q % 2), 176 if q == 1 else 160)

    def rs(p, k, q):
        j, rows = part(q)
        src = k if p else NZ - k
        land = RP if p else RM
        return remote(
            OWN.at[src, j, rows], land.at[k - 1, j, rows],
            rs_send.at[p, k - 1, q], rs_recv.at[p, k - 1, q], zdev(1 if p else -1),
        )

    pl.semaphore_wait(barrier, 7)

    for q in range(4):
        ag(1, 1, q).start()
        ag(0, 1, (q + 2) % 4).start()
    share(0, 0).start()
    share(0, 1).start()
    load_g.wait()
    load_u.wait()

    def rows_of(slots, j, lo):
        top, low = [], []
        for r in slots:
            for buf in (ZR, ZS):
                block = buf[r, j, pl.ds(lo, 80), :].astype(F32)
                top.append(block[:TOK])
                low.append(block[TOK:])
        return jnp.concatenate(top, axis=0), jnp.concatenate(low, axis=0)

    def gather_rows(slots, row0):
        n = 80 * len(slots)
        rows = pl.ds(row0, n)
        for r in slots:
            for j in range(2):
                share(r, j).wait_recv()
        for j in range(2):
            for b in range(4):
                top, low = rows_of(slots, j, 80 * b)
                X[rows, pl.ds(j * 512 + b * 128, 128)] = top.astype(BF16)
                X[rows, pl.ds(1024 + j * 512 + b * 128, 128)] = low.astype(BF16)
        weights = []
        for r in slots:
            for buf in (ZR, ZS):
                tile = buf[r, 0, pl.ds(400, 16), :].astype(F32)
                line = jnp.sum(jnp.where(r16w == z, tile, 0.0), axis=0, keepdims=True)
                weights.append(jnp.sum(jnp.where(pick, line, 0.0), axis=1, keepdims=True))
        return jnp.concatenate(weights, axis=0)

    def units(slots, row0, t, weight):
        rows = pl.ds(row0, 80 * len(slots))
        cot = jnp.concatenate([rows_of(slots, j, 320)[t] for j in range(2)], axis=1)
        xs = X[rows, :]
        gate = dot(xs, WC[:, pl.ds(256 * t, 256)])
        up = dot(xs, WC[:, pl.ds(FF + 256 * t, 256)])
        sig = 1.0 / (1.0 + jnp.exp(-gate))
        act = gate * sig
        ups = weight * cot
        GU[rows, pl.ds(256 * t, 256)] = (
            ups * up * sig * (1.0 + gate * (1.0 - sig))
        ).astype(BF16)
        GU[rows, pl.ds(FF + 256 * t, 256)] = (ups * act).astype(BF16)
        return jnp.sum(act * up * cot, axis=1, keepdims=True)

    def put_sums(slots, total):
        i = 0
        for r in slots:
            for buf in (OWN, SND):
                line = jnp.sum(
                    jnp.where(pick, total[TOK * i:TOK * i + TOK], 0.0), axis=0, keepdims=True
                )
                buf[r, 0, pl.ds(320, 16), :] = jnp.where(r16w == z, line, 0.0).astype(BF16)
                i += 1

    def first(slots, row0, between=None):
        weight = gather_rows(slots, row0)
        total = units(slots, row0, 0, weight)
        if between is not None:
            between()
        put_sums(slots, total + units(slots, row0, 1, weight))

    def second(slots, row0, j):
        grads = GU[pl.ds(row0, 80 * len(slots)), :]
        top = dot(grads, WC[pl.ds(j * 512, 512), :], NT)
        low = dot(grads, WC[pl.ds(1024 + j * 512, 512), :], NT)
        i = 0
        for r in slots:
            for buf in (OWN, SND):
                for b in range(4):
                    buf[r, j, pl.ds(80 * b, 80), :] = jnp.concatenate(
                        [
                            top[TOK * i:TOK * i + TOK, 128 * b:128 * b + 128],
                            low[TOK * i:TOK * i + TOK, 128 * b:128 * b + 128],
                        ],
                        axis=0,
                    ).astype(BF16)
                i += 1
            give(r, j).start()

    def arrive(k, i):
        for p in (1, 0):
            q = i if p else (i + 2) % 4
            ag(p, k, q).wait_recv()
            if i < 2:
                ag(p, k + 1, q).start()
            else:
                @pl.when(k < 5)
                def _():
                    ag(p, k + 1, q).start()
            if i % 2:
                share(NZ - k if p else k, q // 2).start()

    def pair(k):
        return [NZ - k, k], pl.multiple_of(160 * k - 80, 16)

    arrive(1, 0)
    arrive(1, 1)
    first([0], 0, lambda: arrive(1, 2))
    second([0], 0, 0)
    arrive(1, 3)
    second([0], 0, 1)

    def gather_step(k, carry, old=True):
        arrive(k, 0)
        if old:
            second(*pair(k - 2), 1)
        arrive(k, 1)
        first(*pair(k - 1), lambda: arrive(k, 2))
        arrive(k, 3)
        second(*pair(k - 1), 0)
        return carry

    gather_step(2, 0, False)
    lax.fori_loop(3, 6, gather_step, 0)
    for i in range(2):
        for p in (1, 0):
            ag(p, 6, i if p else i + 2).wait_recv()
            if i:
                share(6, 1 - p).start()
        if i == 0:
            second(*pair(4), 1)
    first(*pair(5))
    second(*pair(5), 0)
    second(*pair(5), 1)

    def weight_rows(dy):
        col = pl.multiple_of(lax.rem(y + dy, NY) * 256, 256)
        xs = X[:, pl.ds(col, 256)]
        PA[dy] = dot(xs, GU[:, pl.ds(0, CA)], TN).astype(BF16)
        PB[dy] = dot(xs, GU[:, pl.ds(CA, CB)], TN).astype(BF16)

    def xrow(step):
        return lax.rem(x + step, NX) * 64

    def near(p):
        return 1 if p else NX - 1

    def ax1(p, dy):
        row = pl.multiple_of(xrow(2) + (0 if p else 32), 32)
        return remote(
            PA.at[dy, pl.ds(row, 32)], AX1.at[p, dy], ax1_send.at[p, dy], ax1_recv.at[p, dy],
            xdev(1 if p else -1),
        )

    def ax2(p, dy):
        row = pl.multiple_of(xrow(near(p)), 64)
        return remote(
            PA.at[dy, pl.ds(row, 64)], AX2.at[p, dy], ax2_send.at[p, dy], ax2_recv.at[p, dy],
            xdev(1 if p else -1),
        )

    def a_open(dy):
        weight_rows(dy)
        ax1(1, dy).start()
        ax1(0, dy).start()

    def a_pass(p, dy):
        ax1(p, dy).wait_recv()
        row = pl.multiple_of(xrow(near(p)) + (0 if p else 32), 32)
        PA[dy, pl.ds(row, 32), :] = (
            PA[dy, pl.ds(row, 32), :].astype(F32) + AX1[p, dy].astype(F32)
        ).astype(BF16)
        ax2(p, dy).start()

    def a_sum(dy):
        ax2(1, dy).wait_recv()
        ax2(0, dy).wait_recv()
        row = pl.multiple_of(x * 64, 64)
        SA[dy] = (
            PA[dy, pl.ds(row, 64), :].astype(F32)
            + AX2[1, dy].astype(F32) + AX2[0, dy].astype(F32)
        )
        if dy == 4:
            SAB[4] = SA[4].astype(BF16)
            ay1(1).start()
            ay1(0).start()

    def ay1(p):
        return remote(
            SAB.at[4, pl.ds(0 if p else 32, 32)], AY1.at[p], ay_send.at[p, 3], ay_recv.at[p, 3],
            ydev(1 if p else -1),
        )

    def ay(p, k):
        return remote(
            SAB.at[k if p else NY - k], AY.at[p, k - 1], ay_send.at[p, k - 1],
            ay_recv.at[p, k - 1], ydev(1 if p else -1),
        )

    def ay_pass(p, k):
        dy = k if p else NY - k
        if k == 3:
            ay1(p).wait_recv()
            lo = 0 if p else 32
            SAB[dy, pl.ds(32 - lo, 32), :] = SA[dy, pl.ds(32 - lo, 32), :].astype(BF16)
            SAB[dy, pl.ds(lo, 32), :] = (
                SA[dy, pl.ds(lo, 32), :] + AY1[p].astype(F32)
            ).astype(BF16)
        else:
            ay(p, k + 1).wait_recv()
            SAB[dy] = (SA[dy] + AY[p, k].astype(F32)).astype(BF16)
        ay(p, k).start()

    def a_last():
        ay(1, 1).wait_recv()
        ay(0, 1).wait_recv()
        total = SA[0] + AY[1, 0].astype(F32) + AY[0, 0].astype(F32)
        dg[...] = total[:, :FF]
        du[:, pl.ds(0, CA - FF)] = total[:, FF:]
        stores[2].start()

    def by(p, k, s):
        dy = k if p else NY - k
        return remote(
            PB.at[dy, pl.ds(128 * s, 128)], BY.at[p, k - 1, s], by_send.at[p, k - 1, s],
            by_recv.at[p, k - 1, s], ydev(1 if p else -1),
        )

    def b_pass(p, k, s):
        dy = k if p else NY - k
        rows = pl.ds(128 * s, 128)
        if k < 3 or (k == 3 and s == 1 - p):
            by(p, k + 1, s).wait_recv()
            PB[dy, rows, :] = (PB[dy, rows, :].astype(F32) + BY[p, k, s].astype(F32)).astype(BF16)
        by(p, k, s).start()

    def b_sum():
        for s in (1, 0):
            by(1, 1, s).wait_recv()
            by(0, 1, s).wait_recv()
            rows = pl.ds(128 * s, 128)
            SB[rows, :] = (
                PB[0, rows, :].astype(F32) + BY[1, 0, s].astype(F32) + BY[0, 0, s].astype(F32)
            )
        row = pl.multiple_of(xrow(2), 64)
        SBB[...] = SB[pl.ds(row, 64), :].astype(BF16)
        bx1(1).start()
        bx1(0).start()

    def bx1(p):
        return remote(
            SBB.at[pl.ds(0 if p else 32, 32)], BX1.at[p], bx1_send.at[p], bx1_recv.at[p],
            xdev(1 if p else -1),
        )

    def bx2(p):
        return remote(
            BXS.at[p], BX2.at[p], bx2_send.at[p], bx2_recv.at[p], xdev(1 if p else -1)
        )

    def bx_pass(p):
        row = pl.multiple_of(xrow(near(p)), 64)
        mine = SB[pl.ds(row, 64), :]
        bx1(p).wait_recv()
        lo = 0 if p else 32
        BXS[p, pl.ds(32 - lo, 32), :] = mine[32 - lo:64 - lo].astype(BF16)
        BXS[p, pl.ds(lo, 32), :] = (mine[lo:lo + 32] + BX1[p].astype(F32)).astype(BF16)
        bx2(p).start()

    def b_last():
        bx2(1).wait_recv()
        bx2(0).wait_recv()
        row = pl.multiple_of(x * 64, 64)
        du[:, pl.ds(CA - FF, CB)] = (
            SB[pl.ds(row, 64), :] + BX2[1].astype(F32) + BX2[0].astype(F32)
        )

    given = set()

    def mix(r, q):
        j, rows = part(q)
        if (r, j) not in given:
            given.add((r, j))
            give(r, j).wait_recv()
        return OWN[r, j, rows, :].astype(F32) + SIB[r, j, rows, :].astype(F32)

    def z_pass(p, k, q):
        r = k if p else NZ - k
        j, rows = part(q)
        total = mix(r, q)
        if k < 5 or (k == 5 and j == 1 - p):
            rs(p, k + 1, q).wait_recv()
            land = RP if p else RM
            total = total + land[k, j, rows, :].astype(F32)
        OWN[r, j, rows, :] = total.astype(BF16)
        rs(p, k, q).start()

    def z_last(q):
        j, rows = part(q)
        rs(1, 1, q).wait_recv()
        rs(0, 1, q).wait_recv()
        total = mix(0, q) + RP[0, j, rows, :].astype(F32) + RM[0, j, rows, :].astype(F32)
        for b in range(2):
            lo = j * 512 + (q % 2 * 2 + b) * 128
            gt[:, pl.ds(lo, 128)] = total[80 * b:80 * b + TOK].astype(BF16)
            gt[:, pl.ds(1024 + lo, 128)] = total[80 * b + TOK:80 * b + 80].astype(BF16)
        if q == 1:
            back = total[160:176].astype(BF16)
            for k in range(8):
                gc[k:k + 1, :] = sum(
                    jnp.sum(
                        jnp.where(rt[k:k + 1, :] == 2 * r16 + c, dot(back, spots[c], NT), 0.0),
                        axis=0, keepdims=True,
                    )
                    for c in range(2)
                ).astype(BF16)
            stores[1].start()

    steps = {
        "F6": lambda: first([6], 880),
        "S6": lambda: [second([6], 880, j) for j in range(2)],
        "W": a_open, "A2": a_pass, "A3": a_sum, "AY": ay_pass, "AF": a_last,
        "BY": b_pass, "BS": b_sum, "BX": bx_pass, "BF": b_last,
        "Z": z_pass, "ZF": z_last,
    }
    for name, *where in ORDER:
        steps[name](*where)
    stores[0].start()
    stores[3].start()

    for p in (1, 0):
        for k in range(1, 7):
            for j in range(2):
                if k < 6 or j == 1 - p:
                    for q in (2 * j, 2 * j + 1):
                        ag(p, k, q).wait_send()
                        rs(p, k, q).wait_send()
        for dy in range(NY):
            ax1(p, dy).wait_send()
            ax2(p, dy).wait_send()
        ay1(p).wait_send()
        for k in range(1, 4):
            ay(p, k).wait_send()
            for s in range(2):
                by(p, k, s).wait_send()
        by(p, 4, 1 - p).wait_send()
        bx1(p).wait_send()
        bx2(p).wait_send()
    for r in range(NZ):
        for j in range(2):
            share(r, j).wait_send()
            give(r, j).wait_send()
    for store in stores:
        store.wait()


def hand_on(a, b, c, d, e, f, g, h, va, vb, vc, vd, sem, sem2):
    gets = [
        pltpu.make_async_copy(src, dst, sem.at[i])
        for i, (src, dst) in enumerate(((a, va), (b, vb), (c, vc), (d, vd)))
    ]
    puts = [
        pltpu.make_async_copy(src, dst, sem2.at[i])
        for i, (src, dst) in enumerate(((va, e), (vb, f), (vc, g), (vd, h)))
    ]
    for get in gets:
        get.start()
    for get, put in zip(gets, puts):
        get.wait()
        put.start()
    for put in puts:
        put.wait()


def per_device(tokens, grad_out, routes, combine, w_gate, w_up):
    hbm = pl.BlockSpec(memory_space=pl.ANY)
    V = pltpu.VMEM
    S = pltpu.SemaphoreType.DMA
    shapes = (
        jax.ShapeDtypeStruct((TOK, DM), BF16),
        jax.ShapeDtypeStruct((8, TOK), BF16),
        jax.ShapeDtypeStruct((64, FF), F32),
        jax.ShapeDtypeStruct((64, FF), F32),
    )
    out = pl.pallas_call(
        kernel,
        out_shape=shapes,
        in_specs=[hbm] * 6,
        out_specs=(hbm,) * 4,
        scratch_shapes=[
            V((TOK, DM), BF16),
            V((TOK, FF), BF16),
            V((8, TOK), jnp.int32),
            V((8, TOK), BF16),
            V((TOK, DM), BF16),
            V((8, TOK), BF16),
            V((64, FF), F32),
            V((64, FF), F32),
            V((NZ, 2, 416, 128), BF16),
            V((NZ, 2, 416, 128), BF16),
            V((NZ * 80, DM), BF16),
            V((NZ * 80, 2 * FF), BF16),
            V((DM, 2 * FF), BF16),
            V((NZ, 2, 336, 128), BF16),
            V((NZ, 2, 336, 128), BF16),
            V((NZ, 2, 336, 128), BF16),
            V((6, 2, 336, 128), BF16),
            V((6, 2, 336, 128), BF16),
            V((NY, 256, CA), BF16),
            V((NY, 256, CB), BF16),
            V((2, NY, 32, CA), BF16),
            V((2, NY, 64, CA), BF16),
            V((NY, 64, CA), F32),
            V((NY, 64, CA), BF16),
            V((2, 32, CA), BF16),
            V((2, 3, 64, CA), BF16),
            V((2, 4, 2, 128, CB), BF16),
            V((256, CB), F32),
            V((64, CB), BF16),
            V((2, 32, CB), BF16),
            V((2, 64, CB), BF16),
            V((2, 64, CB), BF16),
            S((2,)), S((4,)), S((4,)),
            S((2, 6, 4)), S((NZ, 4)), S((NZ, 2)), S((NZ, 2)), S((NZ, 2)), S((NZ, 2)),
            S((2, 6, 4)), S((2, 6, 4)),
            S((2, NY)), S((2, NY)), S((2, NY)), S((2, NY)), S((2, 4)), S((2, 4)),
            S((2, 4, 2)), S((2, 4, 2)),
            S((2,)), S((2,)), S((2,)), S((2,)),
        ],
        compiler_params=pltpu.CompilerParams(
            collective_id=0, has_side_effects=True, vmem_limit_bytes=56 * 2**20
        ),
    )(tokens, grad_out, routes.T, combine.T, w_gate, w_up)
    out = pl.pallas_call(
        hand_on,
        out_shape=shapes,
        in_specs=[hbm] * 4,
        out_specs=(hbm,) * 4,
        scratch_shapes=[V(x.shape, x.dtype) for x in shapes] + [S((4,)), S((4,))],
    )(*out)
    return out[0], out[1].T, out[2][None], out[3][None]


def solution(mesh):
    return jax.shard_map(
        per_device,
        mesh=mesh,
        in_specs=(
            P(("dp", "expert"), None),
            P(("dp", "expert"), None),
            P(("dp", "expert"), None),
            P(("dp", "expert"), None),
            P("expert", None, None),
            P("expert", None, None),
        ),
        out_specs=(
            P(("dp", "expert"), None),
            P(("dp", "expert"), None),
            P("expert", "dp", None),
            P("expert", "dp", None),
        ),
        check_vma=False,
    )
```

time: 95.7 us -> 84.9 us (0.89)
  the two profiles are of different devices: /device:TPU:16 before, /device:TPU:2 now
where the time goes in v2:
time: 84.9 us; the launch traced here: 84.7 us
  Pallas kernels  83.9 us (99%)
    pallas_call x1, Pallas kernels, per_device(): pl.pallas_call(kernel, out_shape=shapes, in_specs=[hbm] * 6, out_specs=(h...  82.2 us
    pallas_call x1, Pallas kernels, per_device(): pl.pallas_call(hand_on, out_shape=shapes, in_specs=[hbm] * 4, out_specs=(...  1.78 us

profile of v2, /device:TPU:2, one launch (start us, length us, event | category | flops | bytes accessed | tf_op | source)
XLA Modules:
  0.0 84.7 jit_solution(18381217735135780346)
XLA Ops:
  0.6 82.2 %shard_map.93 = (bf16[40,2048]{1,0:T(8,128)(2,1)}, bf16[8,40]{1,0:T(8,128)(2,1)}, f32[64,512]{1,0:T(8,128)}, f32[64,512]{1,0:T(8,128)}) custom-call(bf16[40,2048]{1,0:T(8,128)(2,1)} %tok_in.1, bf16[40,512]{1,0:T(8,128)(2,1)} %go_in.1, s32[8,40]{1,0:T(8,128)} %bitcast.5, bf16[8,40]{1,0:T(8,128)(2,1)} %bitcast.6, bf16[1,2048,512]{2,1,0:T(8,128)(2,1)} %wg.1, ...), custom_call_target="tpu_custom_call" | custom-call | tf_op jit(solution)/shard_map/pallas_call | solution.py:553
  82.8 1.8 %shard_map.94 = (bf16[40,2048]{1,0:T(8,128)(2,1)}, bf16[8,40]{1,0:T(8,128)(2,1)}, f32[64,512]{1,0:T(8,128)}, f32[64,512]{1,0:T(8,128)}) custom-call(bf16[40,2048]{1,0:T(8,128)(2,1)} %get-tuple-element.12.a, bf16[8,40]{1,0:T(8,128)(2,1)} %get-tuple-element.13.b, f32[64,512]{1,0:T(8,128)} %get-tuple-element.14.c, f32[64,512]{1,0:T(8,128)} %get-tuple-element.15.d), custom_call_target="tpu_custom_call" | custom-call | tf_op jit(solution)/shard_map/pallas_call | solution.py:602

commit v3 on v2

--- a/solution.py
+++ b/solution.py
@@ -20,24 +20,24 @@
 CA = 640
 CB = 2 * FF - CA
 ORDER = (
-    ("F6",), ("W", 4), ("BY", 1, 4, 0), ("BY", 0, 4, 1), ("S6",), ("W", 3), ("W", 5),
-    ("A2", 1, 4), ("A2", 0, 4), ("BY", 1, 3, 1), ("BY", 0, 3, 0), ("Z", 1, 6, 1), ("Z", 1, 6, 0),
-    ("Z", 0, 6, 2), ("Z", 0, 6, 3), ("BY", 1, 3, 0), ("BY", 0, 3, 1), ("W", 2), ("W", 6),
-    ("A2", 1, 3), ("A2", 0, 3), ("A2", 1, 5), ("A2", 0, 5), ("Z", 1, 5, 1), ("Z", 0, 5, 1),
-    ("Z", 1, 5, 0), ("Z", 1, 5, 2), ("Z", 1, 5, 3), ("Z", 0, 5, 0), ("Z", 0, 5, 2),
-    ("Z", 0, 5, 3), ("A3", 4), ("BY", 1, 2, 1), ("BY", 0, 2, 0), ("W", 1), ("BY", 1, 2, 0),
-    ("BY", 0, 2, 1), ("Z", 1, 4, 1), ("Z", 0, 4, 1), ("W", 7), ("Z", 1, 4, 0), ("Z", 0, 4, 0),
-    ("A3", 3), ("Z", 1, 4, 2), ("Z", 0, 4, 2), ("A2", 1, 2), ("A2", 0, 2), ("A2", 1, 6),
-    ("A2", 0, 6), ("Z", 1, 4, 3), ("Z", 0, 4, 3), ("A3", 5), ("AY", 1, 3), ("AY", 0, 3),
-    ("BY", 1, 1, 1), ("BY", 0, 1, 0), ("Z", 1, 3, 1), ("Z", 0, 3, 1), ("W", 0), ("Z", 1, 3, 0),
-    ("Z", 0, 3, 0), ("BY", 1, 1, 0), ("BY", 0, 1, 1), ("Z", 1, 3, 2), ("Z", 0, 3, 2),
-    ("A2", 1, 1), ("A2", 0, 1), ("A3", 2), ("Z", 1, 3, 3), ("Z", 0, 3, 3), ("A2", 1, 7),
-    ("A2", 0, 7), ("AY", 1, 2), ("Z", 1, 2, 1), ("Z", 0, 2, 1), ("A3", 6), ("AY", 0, 2),
-    ("Z", 1, 2, 0), ("Z", 0, 2, 0), ("A2", 1, 0), ("A2", 0, 0), ("Z", 1, 2, 2), ("Z", 0, 2, 2),
-    ("Z", 1, 2, 3), ("Z", 0, 2, 3), ("A3", 1), ("Z", 1, 1, 1), ("Z", 0, 1, 1), ("BS",),
-    ("Z", 1, 1, 0), ("Z", 0, 1, 0), ("A3", 7), ("Z", 1, 1, 2), ("Z", 0, 1, 2), ("AY", 1, 1),
-    ("AY", 0, 1), ("Z", 1, 1, 3), ("Z", 0, 1, 3), ("A3", 0), ("BX", 1), ("BX", 0), ("ZF", 1),
-    ("ZF", 0), ("ZF", 2), ("AF",), ("ZF", 3), ("BF",),
+    ("F5",), ("S5", 1), ("F6",), ("W", 4), ("BY", 0, 4, 1), ("BY", 1, 4, 0), ("S6", 0), ("S6", 1),
+    ("W", 3), ("BY", 1, 3, 1), ("W", 5), ("BY", 0, 3, 0), ("S5", 0), ("Z", 1, 6, 1), ("A2", 0, 4),
+    ("A2", 1, 4), ("Z", 1, 6, 0), ("Z", 0, 6, 3), ("Z", 1, 5, 2), ("Z", 0, 6, 2), ("W", 2),
+    ("BY", 1, 3, 0), ("BY", 0, 3, 1), ("Z", 1, 5, 3), ("A2", 0, 3), ("Z", 0, 5, 0), ("A2", 1, 5),
+    ("Z", 0, 5, 1), ("W", 6), ("BY", 1, 2, 1), ("Z", 1, 5, 1), ("BY", 0, 2, 0), ("Z", 0, 5, 3),
+    ("A2", 1, 3), ("A2", 0, 5), ("Z", 1, 5, 0), ("A3", 4), ("Z", 0, 5, 2), ("Z", 1, 4, 2),
+    ("W", 1), ("Z", 0, 4, 0), ("BY", 1, 2, 0), ("A2", 1, 2), ("Z", 1, 4, 3), ("BY", 0, 2, 1),
+    ("Z", 0, 4, 1), ("Z", 1, 4, 1), ("A2", 0, 2), ("Z", 0, 4, 3), ("W", 7), ("Z", 1, 4, 0),
+    ("BY", 1, 1, 1), ("BY", 0, 1, 0), ("Z", 0, 4, 2), ("Z", 1, 3, 2), ("Z", 0, 3, 0), ("A3", 3),
+    ("AY", 1, 3), ("A2", 0, 6), ("Z", 1, 3, 3), ("A2", 1, 6), ("Z", 0, 3, 1), ("A3", 5),
+    ("A2", 1, 1), ("AY", 0, 3), ("Z", 1, 3, 1), ("Z", 0, 3, 3), ("W", 0), ("Z", 1, 3, 0),
+    ("BY", 1, 1, 0), ("BY", 0, 1, 1), ("Z", 0, 3, 2), ("A2", 0, 1), ("A2", 1, 7), ("Z", 1, 2, 2),
+    ("Z", 0, 2, 0), ("Z", 1, 2, 3), ("A3", 2), ("Z", 0, 2, 1), ("A2", 0, 7), ("A3", 6),
+    ("Z", 1, 2, 1), ("AY", 1, 2), ("AY", 0, 2), ("Z", 0, 2, 3), ("Z", 1, 2, 0), ("Z", 0, 2, 2),
+    ("Z", 1, 1, 2), ("Z", 0, 1, 0), ("BS",), ("Z", 1, 1, 3), ("A2", 0, 0), ("Z", 0, 1, 1),
+    ("A3", 1), ("Z", 1, 1, 1), ("A2", 1, 0), ("A3", 7), ("AY", 1, 1), ("AY", 0, 1),
+    ("Z", 0, 1, 3), ("Z", 1, 1, 0), ("Z", 0, 1, 2), ("BX", 1), ("BX", 0), ("ZF", 1), ("ZF", 3),
+    ("A3", 0), ("ZF", 0), ("AF",), ("ZF", 2), ("BF",),
 )
 NT = (((1,), (1,)), ((), ()))
 TN = (((0,), (0,)), ((), ()))
@@ -119,6 +119,42 @@
             [gf[:, j * 128:j * 128 + 128], gf[:, 256 + j * 128:256 + j * 128 + 128]], axis=0
         ).astype(BF16)
 
+    def ag(p, k, q):
+        j, h = q // 2, q % 2
+        rows = pl.ds(208 * h, AG_ROWS[j] - 208 if h else 208)
+        if p:
+            src, dst = lax.rem(13 - k, NZ), NZ - k
+        else:
+            src, dst = k - 1, k
+        return remote(
+            ZR.at[src, j, rows], ZR.at[dst, j, rows],
+            ag_send.at[p, k - 1, q], zr_recv.at[dst, q], zdev(1 if p else -1),
+        )
+
+    def share(r, j):
+        rows = pl.ds(0, AG_ROWS[j])
+        return remote(ZR.at[r, j, rows], ZS.at[r, j, rows], sf_send.at[r, j], zs_recv.at[r, j], sib)
+
+    def give(r, j):
+        rows = pl.ds(0, RS_ROWS[j])
+        return remote(SND.at[r, j, rows], SIB.at[r, j, rows], snd_send.at[r, j], sib_recv.at[r, j], sib)
+
+    def part(q):
+        return q // 2, pl.ds(160 * (q % 2), 176 if q == 1 else 160)
+
+    def rs(p, k, q):
+        j, rows = part(q)
+        src = k if p else NZ - k
+        land = RP if p else RM
+        return remote(
+            OWN.at[src, j, rows], land.at[k - 1, j, rows],
+            rs_send.at[p, k - 1, q], rs_recv.at[p, k - 1, q], zdev(1 if p else -1),
+        )
+
+    pl.semaphore_wait(barrier, 7)
+    ag(1, 1, 0).start()
+    ag(0, 1, 2).start()
+
     rt = routes[...]
     cf = comb[...].astype(F32)
     r16, r40 = iota((16, TOK), 0), iota((TOK, 128), 0)
@@ -135,41 +171,7 @@
 
     pick = lane == core * TOK + r40
 
-    def ag(p, k, q):
-        j, h = q // 2, q % 2
-        rows = pl.ds(208 * h, AG_ROWS[j] - 208 if h else 208)
-        if p:
-            src, dst = lax.rem(13 - k, NZ), NZ - k
-        else:
-            src, dst = k - 1, k
-        return remote(
-            ZR.at[src, j, rows], ZR.at[dst, j, rows],
-            ag_send.at[p, k - 1, q], zr_recv.at[dst, q], zdev(1 if p else -1),
-        )
-
-    def share(r, j):
-        rows = pl.ds(0, AG_ROWS[j])
-        return remote(ZR.at[r, j, rows], ZS.at[r, j, rows], sf_send.at[r, j], zs_recv.at[r, j], sib)
-
-    def give(r, j):
-        rows = pl.ds(0, RS_ROWS[j])
-        return remote(SND.at[r, j, rows], SIB.at[r, j, rows], snd_send.at[r, j], sib_recv.at[r, j], sib)
-
-    def part(q):
-        return q // 2, pl.ds(160 * (q % 2), 176 if q == 1 else 160)
-
-    def rs(p, k, q):
-        j, rows = part(q)
-        src = k if p else NZ - k
-        land = RP if p else RM
-        return remote(
-            OWN.at[src, j, rows], land.at[k - 1, j, rows],
-            rs_send.at[p, k - 1, q], rs_recv.at[p, k - 1, q], zdev(1 if p else -1),
-        )
-
-    pl.semaphore_wait(barrier, 7)
-
-    for q in range(4):
+    for q in range(1, 4):
         ag(1, 1, q).start()
         ag(0, 1, (q + 2) % 4).start()
     share(0, 0).start()
@@ -297,9 +299,6 @@
                 share(6, 1 - p).start()
         if i == 0:
             second(*pair(4), 1)
-    first(*pair(5))
-    second(*pair(5), 0)
-    second(*pair(5), 1)
 
     def weight_rows(dy):
         col = pl.multiple_of(lax.rem(y + dy, NY) * 256, 256)
@@ -485,8 +484,10 @@
             stores[1].start()
 
     steps = {
+        "F5": lambda: first(*pair(5)),
+        "S5": lambda j: second(*pair(5), j),
         "F6": lambda: first([6], 880),
-        "S6": lambda: [second([6], 880, j) for j in range(2)],
+        "S6": lambda j: second([6], 880, j),
         "W": a_open, "A2": a_pass, "A3": a_sum, "AY": ay_pass, "AF": a_last,
         "BY": b_pass, "BS": b_sum, "BX": bx_pass, "BF": b_last,
         "Z": z_pass, "ZF": z_last,
@@ -553,7 +554,7 @@
     out = pl.pallas_call(
         kernel,
         out_shape=shapes,
-        in_specs=[hbm] * 6,
+        in_specs=[pl.BlockSpec(memory_space=pltpu.HBM)] * 6,
         out_specs=(hbm,) * 4,
         scratch_shapes=[
             V((TOK, DM), BF16),

time: 84.9 us -> 83.1 us (0.979)
  Pallas kernels: 83.9 us -> 82.1 us
    pallas_call x1, Pallas kernels: 82.2 us -> 80.4 us  [per_device(): pl.pallas_call(kernel, out_shape=shapes, in_specs=[pl.BlockSpec(memory_sp...]
where the time goes in v3:
time: 83.1 us; the launch traced here: 82.9 us
  Pallas kernels  82.1 us (99%)
    pallas_call x1, Pallas kernels, per_device(): pl.pallas_call(kernel, out_shape=shapes, in_specs=[pl.BlockSpec(memory_sp...  80.4 us
    pallas_call x1, Pallas kernels, per_device(): pl.pallas_call(hand_on, out_shape=shapes, in_specs=[hbm] * 4, out_specs=(...  1.78 us

profile of v3, /device:TPU:2, one launch (start us, length us, event | category | flops | bytes accessed | tf_op | source)
XLA Modules:
  0.0 82.9 jit_solution(17169140362594417809)
XLA Ops:
  0.6 80.4 %shard_map.93 = (bf16[40,2048]{1,0:T(8,128)(2,1)}, bf16[8,40]{1,0:T(8,128)(2,1)}, f32[64,512]{1,0:T(8,128)}, f32[64,512]{1,0:T(8,128)}) custom-call(bf16[40,2048]{1,0:T(8,128)(2,1)} %tok_in.1, bf16[40,512]{1,0:T(8,128)(2,1)} %go_in.1, s32[8,40]{1,0:T(8,128)} %bitcast.5, bf16[8,40]{1,0:T(8,128)(2,1)} %bitcast.6, bf16[1,2048,512]{2,1,0:T(8,128)(2,1)} %wg.1, ...), custom_call_target="tpu_custom_call" | custom-call | tf_op jit(solution)/shard_map/pallas_call | solution.py:554
  81.0 1.8 %shard_map.94 = (bf16[40,2048]{1,0:T(8,128)(2,1)}, bf16[8,40]{1,0:T(8,128)(2,1)}, f32[64,512]{1,0:T(8,128)}, f32[64,512]{1,0:T(8,128)}) custom-call(bf16[40,2048]{1,0:T(8,128)(2,1)} %get-tuple-element.12.a, bf16[8,40]{1,0:T(8,128)(2,1)} %get-tuple-element.13.b, f32[64,512]{1,0:T(8,128)} %get-tuple-element.14.c, f32[64,512]{1,0:T(8,128)} %get-tuple-element.15.d), custom_call_target="tpu_custom_call" | custom-call | tf_op jit(solution)/shard_map/pallas_call | solution.py:603

commit v4 on v3

--- a/solution.py
+++ b/solution.py
@@ -300,6 +300,12 @@
         if i == 0:
             second(*pair(4), 1)
 
+    sent, done = [], []
+
+    def go(copy):
+        copy.start()
+        sent.append((len(done), copy))
+
     def weight_rows(dy):
         col = pl.multiple_of(lax.rem(y + dy, NY) * 256, 256)
         xs = X[:, pl.ds(col, 256)]
@@ -328,8 +334,8 @@
 
     def a_open(dy):
         weight_rows(dy)
-        ax1(1, dy).start()
-        ax1(0, dy).start()
+        go(ax1(1, dy))
+        go(ax1(0, dy))
 
     def a_pass(p, dy):
         ax1(p, dy).wait_recv()
@@ -337,7 +343,7 @@
         PA[dy, pl.ds(row, 32), :] = (
             PA[dy, pl.ds(row, 32), :].astype(F32) + AX1[p, dy].astype(F32)
         ).astype(BF16)
-        ax2(p, dy).start()
+        go(ax2(p, dy))
 
     def a_sum(dy):
         ax2(1, dy).wait_recv()
@@ -349,8 +355,8 @@
         )
         if dy == 4:
             SAB[4] = SA[4].astype(BF16)
-            ay1(1).start()
-            ay1(0).start()
+            go(ay1(1))
+            go(ay1(0))
 
     def ay1(p):
         return remote(
@@ -376,7 +382,7 @@
         else:
             ay(p, k + 1).wait_recv()
             SAB[dy] = (SA[dy] + AY[p, k].astype(F32)).astype(BF16)
-        ay(p, k).start()
+        go(ay(p, k))
 
     def a_last():
         ay(1, 1).wait_recv()
@@ -399,7 +405,7 @@
         if k < 3 or (k == 3 and s == 1 - p):
             by(p, k + 1, s).wait_recv()
             PB[dy, rows, :] = (PB[dy, rows, :].astype(F32) + BY[p, k, s].astype(F32)).astype(BF16)
-        by(p, k, s).start()
+        go(by(p, k, s))
 
     def b_sum():
         for s in (1, 0):
@@ -411,8 +417,8 @@
             )
         row = pl.multiple_of(xrow(2), 64)
         SBB[...] = SB[pl.ds(row, 64), :].astype(BF16)
-        bx1(1).start()
-        bx1(0).start()
+        go(bx1(1))
+        go(bx1(0))
 
     def bx1(p):
         return remote(
@@ -432,7 +438,7 @@
         lo = 0 if p else 32
         BXS[p, pl.ds(32 - lo, 32), :] = mine[32 - lo:64 - lo].astype(BF16)
         BXS[p, pl.ds(lo, 32), :] = (mine[lo:lo + 32] + BX1[p].astype(F32)).astype(BF16)
-        bx2(p).start()
+        go(bx2(p))
 
     def b_last():
         bx2(1).wait_recv()
@@ -460,7 +466,7 @@
             land = RP if p else RM
             total = total + land[k, j, rows, :].astype(F32)
         OWN[r, j, rows, :] = total.astype(BF16)
-        rs(p, k, q).start()
+        go(rs(p, k, q))
 
     def z_last(q):
         j, rows = part(q)
@@ -492,33 +498,24 @@
         "BY": b_pass, "BS": b_sum, "BX": bx_pass, "BF": b_last,
         "Z": z_pass, "ZF": z_last,
     }
+    early = [ag(p, k, q) for k in range(1, 7) for p in (1, 0) for q in range(4)
+             if k < 6 or q // 2 == 1 - p]
+    early += [share(r, j) for r in range(NZ) for j in range(2)]
+    early += [give(r, j) for r in (0, 1, 11, 2, 10, 3, 9, 4, 8, 5, 7, 6) for j in range(2)]
     for name, *where in ORDER:
         steps[name](*where)
+        done.append(name)
+        if len(done) > 25:
+            for copy in early[:2]:
+                copy.wait_send()
+            early = early[2:]
+        while sent and sent[0][0] < len(done) - 55:
+            sent.pop(0)[1].wait_send()
     stores[0].start()
     stores[3].start()
 
-    for p in (1, 0):
-        for k in range(1, 7):
-            for j in range(2):
-                if k < 6 or j == 1 - p:
-                    for q in (2 * j, 2 * j + 1):
-                        ag(p, k, q).wait_send()
-                        rs(p, k, q).wait_send()
-        for dy in range(NY):
-            ax1(p, dy).wait_send()
-            ax2(p, dy).wait_send()
-        ay1(p).wait_send()
-        for k in range(1, 4):
-            ay(p, k).wait_send()
-            for s in range(2):
-                by(p, k, s).wait_send()
-        by(p, 4, 1 - p).wait_send()
-        bx1(p).wait_send()
-        bx2(p).wait_send()
-    for r in range(NZ):
-        for j in range(2):
-            share(r, j).wait_send()
-            give(r, j).wait_send()
+    for copy in early + [copy for _, copy in sent]:
+        copy.wait_send()
     for store in stores:
         store.wait()
 

time: 83.1 us -> 83.1 us (level)
  no operation moved by 1% of the time
where the time goes in v4:
time: 83.1 us; the launch traced here: 82.9 us
  Pallas kernels  82.1 us (99%)
    pallas_call x1, Pallas kernels, per_device(): pl.pallas_call(kernel, out_shape=shapes, in_specs=[pl.BlockSpec(memory_sp...  80.4 us
    pallas_call x1, Pallas kernels, per_device(): pl.pallas_call(hand_on, out_shape=shapes, in_specs=[hbm] * 4, out_specs=(...  1.78 us

profile of v4, /device:TPU:2, one launch (start us, length us, event | category | flops | bytes accessed | tf_op | source)
XLA Modules:
  0.0 82.9 jit_solution(7421862974152528943)
XLA Ops:
  0.6 80.4 %shard_map.93 = (bf16[40,2048]{1,0:T(8,128)(2,1)}, bf16[8,40]{1,0:T(8,128)(2,1)}, f32[64,512]{1,0:T(8,128)}, f32[64,512]{1,0:T(8,128)}) custom-call(bf16[40,2048]{1,0:T(8,128)(2,1)} %tok_in.1, bf16[40,512]{1,0:T(8,128)(2,1)} %go_in.1, s32[8,40]{1,0:T(8,128)} %bitcast.5, bf16[8,40]{1,0:T(8,128)(2,1)} %bitcast.6, bf16[1,2048,512]{2,1,0:T(8,128)(2,1)} %wg.1, ...), custom_call_target="tpu_custom_call" | custom-call | tf_op jit(solution)/shard_map/pallas_call | solution.py:551
  81.0 1.8 %shard_map.94 = (bf16[40,2048]{1,0:T(8,128)(2,1)}, bf16[8,40]{1,0:T(8,128)(2,1)}, f32[64,512]{1,0:T(8,128)}, f32[64,512]{1,0:T(8,128)}) custom-call(bf16[40,2048]{1,0:T(8,128)(2,1)} %get-tuple-element.12.a, bf16[8,40]{1,0:T(8,128)(2,1)} %get-tuple-element.13.b, f32[64,512]{1,0:T(8,128)} %get-tuple-element.14.c, f32[64,512]{1,0:T(8,128)} %get-tuple-element.15.d), custom_call_target="tpu_custom_call" | custom-call | tf_op jit(solution)/shard_map/pallas_call | solution.py:600
